TPU v7x, 256 devices: a whole 4x4x8 slice. The times are simulated.
256 devices in a mesh: shot: 32 (over z, y_hi, core), surf: 8 (over x, y_lo).
Axes of the slice: x: 4, y: 4 (y_hi: 2, y_lo: 2; y = y_hi * 2 + y_lo), z: 8, core: 2. Of those that a mesh axis runs over, the one named last changes fastest.
Arguments:
- data: float32 [64, 512, 512], P('shot', 'surf'), may hold values from -6 to 6
- positions: int32 [512], P('surf'), may hold values from 0 to 255, as said below
- plan: int32 [32], replicated, may hold values from 0 to 31, each once
- primaries: bfloat16 [256, 16, 32, 256], P('surf', None, 'shot'), may hold values from -0.015625 to 0.015625
- scale: float32 [64], P('shot'), may hold values from 0.5 to 1.5
Outputs:
- demultiplied: float32 [64, 512, 512], P('shot', 'surf')
Inputs may be any that keep to these rules, and one draw needn't show every extreme that they name: `positions`: receiver r lies at a position of the block [b * 32, (b + 1) * 32) with b = r // 64; in each such block of receivers the first maps to the block's first position and the last to its last. A permutation: slot i of primaries holds receiver panel plan[i].
All inputs are finite; a program needn't handle non-finite values.
Results may differ from a plain program's by a relative error of at most 0.0065.
Values may be sent and summed in bfloat16 or wider, within the bound.
No kernel may reach another device: no remote copies, remote signals or barrier semaphores. Data moves between devices by JAX's collectives and lax.ppermute only.
A program may use at most 128 MiB of HBM per device.

v0:
```python
import math

import jax
import jax.numpy as jnp
from jax import lax
from jax.sharding import PartitionSpec as P


def fourier_matrices(samples):
    length = 2 * samples
    time_index = jnp.arange(samples, dtype=jnp.int32)
    phase_index = time_index[:, None] * time_index[None, :] % length
    angles = phase_index.astype(jnp.float32) * (2.0 * math.pi / length)
    cosine = jnp.cos(angles)
    sine_part = jnp.sin(angles)
    alternate = (1 - 2 * (time_index % 2)).astype(jnp.float32)
    nyquist = time_index == 0
    forward_imag = jnp.where(nyquist[None, :], alternate[:, None], -sine_part)
    forward = jnp.concatenate([cosine, forward_imag], axis=1).astype(jnp.bfloat16)
    weights = jnp.where(nyquist, 1.0, 2.0).astype(jnp.float32) / length
    backward_real_table = cosine.T * weights[:, None]
    inverse_imag = jnp.where(
        nyquist[:, None], alternate[None, :] / length, -2.0 * sine_part.T / length
    )
    inverse = jnp.concatenate([backward_real_table, inverse_imag], axis=0).astype(jnp.bfloat16)
    return (forward, inverse)


def spectral_product(left, right):
    half = left.shape[-1] // 2
    left_real = left[..., :half]
    left_imag = left[..., half:]
    right_real = right[..., :half]
    right_imag = right[..., half:]

    def contract(leading_factor, trailing_factor):
        return jnp.einsum(
            "quw,ugw->qgw", leading_factor, trailing_factor, preferred_element_type=jnp.float32
        )

    real_cross_term = contract(left_real, right_real)
    imaginary_cross_term = contract(left_imag, right_imag)
    crossed = contract(left_real, right_imag) + contract(left_imag, right_real)
    interior = (jnp.arange(half) > 0).astype(jnp.float32)
    return jnp.concatenate(
        [
            real_cross_term - interior * imaginary_cross_term,
            interior * crossed + (1.0 - interior) * imaginary_cross_term,
        ],
        axis=-1,
    )


def on_device(data, positions, plan, primaries, scale):
    shot_count, receiver_count, samples = data.shape
    position_count = primaries.shape[0]
    panel_width = primaries.shape[1]
    tap_count = primaries.shape[3]
    forward, inverse = fourier_matrices(samples)
    local_index = positions - lax.axis_index("surf") * position_count
    onehot = (local_index[:, None] == jnp.arange(position_count, dtype=jnp.int32)[None, :]).astype(
        jnp.float32
    )
    gathered = jnp.einsum("srt,rx->sxt", data, onehot, precision=lax.Precision.HIGHEST).astype(
        jnp.bfloat16
    )
    panel_order = jnp.argsort(plan)
    own_spectra = jnp.dot(
        primaries.reshape(-1, tap_count), forward[:tap_count], preferred_element_type=jnp.float32
    )
    own_spectra = own_spectra.astype(jnp.bfloat16).reshape(position_count, panel_width, 2 * samples)
    piece_rows = lax.all_gather(gathered, "shot", axis=0, tiled=True)
    piece_count = piece_rows.shape[0]
    spectrum = jnp.dot(piece_rows.reshape(-1, samples), forward, preferred_element_type=jnp.float32)
    spectrum = spectrum.astype(jnp.bfloat16).reshape(piece_count, position_count, 2 * samples)
    partial_value = spectral_product(spectrum, own_spectra)
    summed = lax.psum_scatter(
        partial_value.astype(jnp.bfloat16), "surf", scatter_dimension=1, tiled=True
    ).astype(jnp.float32)
    rows_kept = summed.shape[1]
    spectrum = summed.astype(jnp.bfloat16)
    in_time = jnp.dot(
        spectrum.reshape(-1, 2 * samples), inverse, preferred_element_type=jnp.float32
    )
    in_time = in_time.reshape(summed.shape[0], rows_kept, 1, samples)
    arrived = lax.all_to_all(in_time, "shot", split_axis=0, concat_axis=2, tiled=True)
    ordered = jnp.take(arrived, panel_order, axis=2)
    prediction = ordered.reshape(shot_count, receiver_count, samples)
    return data - scale[:, None, None] * prediction


def solution(mesh):
    in_specs = (P("shot", "surf", None), P("surf"), P(), P("surf", None, "shot", None), P("shot"))
    out_specs = P("shot", "surf", None)
    return jax.shard_map(
        on_device, mesh=mesh, in_specs=in_specs, out_specs=out_specs, check_vma=False
    )
```

profile of v0, /device:TPU:1, one launch (start us, length us, event | category | flops | bytes accessed | tf_op | source)
XLA Modules:
  0.0 220.8 jit_solution(17867552088840173272)
XLA Ops:
  7.2 1.8 fusion.2
  9.2 3.9 %fusion.19 = bf16[512,512]{1,0:T(8,128)(2,1)S(1)} fusion(), kind=kLoop, calls=%fused_computation.34 | loop fusion | flops 3932160 | bytes 524288 | tf_op jit(solution)/shard_map/convert.6
  13.1 5.0 %select_convert_fusion = (bf16[512,512]{1,0:T(8,128)(2,1)}, bf16[512,512]{1,0:T(8,128)(2,1)S(1)}) fusion(bf16[512]{0:T(512)(128)(2,1)S(1)} %broadcast_multiply_fusion, pred[512]{0:T(512)(128)(4,1)S(1)} %iota_compare_fusion.2, bf16[512]{0:T(512)(128)(2,1)S(1)} %fusion.27), kind=kLoop, calls=%fused_computation.23 | loop fusion | flops 4718592 | bytes 1051136 | tf_op jit(solution)/shard_map/convert.1
  18.6 0.9 fusion.36
  19.5 3.8 %copy.17 = bf16[32,16,512]{0,1,2:T(8,128)(2,1)S(1)} copy(bf16[32,16,512]{2,1,0:T(8,128)(2,1)} %get-tuple-element.10) | data formatting | bytes 1048576
  23.3 3.0 %copy.15 = bf16[32,16,512]{0,1,2:T(8,128)(2,1)} copy(bf16[32,16,512]{2,1,0:T(8,128)(2,1)S(1)} %get-tuple-element.9) | data formatting | bytes 1048576 | tf_op jit(solution)/shard_map/slice | solution.py:33
  26.3 68.0 %all-gather.2.cloned.1.call-done = bf16[64,32,512]{2,1,0:T(8,128)(2,1)} async-done(((bf16[2,32,512]{2,1,0:T(8,128)(2,1)}), bf16[64,32,512]{2,1,0:T(8,128)(2,1)}) %all-gather.2.cloned.1.call-update) | async-done | bytes 2097168 | tf_op jit(solution)/shard_map/all_gather | solution.py:72
  94.4 4.0 %convolution_convert_fusion = bf16[2048,1024]{1,0:T(8,128)(2,1)S(1)} fusion(bf16[2048,512]{1,0:T(8,128)(2,1)} %bitcast.49, bf16[512,512]{1,0:T(8,128)(2,1)S(1)} %get-tuple-element.12, bf16[512,512]{1,0:T(8,128)(2,1)} %copy-done.4), kind=kOutput, calls=%fused_computation.4 | convolution fusion | flops 2151677952 | bytes 7340032 | tf_op jit(solution)/shard_map/dot_general | solution.py:74
  98.4 2.5 %fusion.35 = (bf16[64,32,512]{2,1,0:T(8,128)(2,1)}, bf16[64,32,512]{2,1,0:T(8,128)(2,1)}) fusion(bf16[64,32,1024]{2,1,0:T(8,128)(2,1)S(1)} %bitcast.45), kind=kLoop, calls=%fused_computation.62 | loop fusion | bytes 8388608 | tf_op jit(solution)/shard_map/slice | solution.py:31
  100.8 8.8 %copy.18 = bf16[64,32,512]{0,1,2:T(8,128)(2,1)} copy(bf16[64,32,512]{2,1,0:T(8,128)(2,1)} %get-tuple-element.8) | data formatting | bytes 4194304
  109.6 8.8 %copy.16 = bf16[64,32,512]{0,1,2:T(8,128)(2,1)} copy(bf16[64,32,512]{2,1,0:T(8,128)(2,1)} %get-tuple-element.7) | data formatting | bytes 4194304 | tf_op jit(solution)/shard_map/slice | solution.py:31
  118.4 3.6 %fusion.37 = f32[512,16,64]{2,1,0:T(8,128)S(1)} fusion(bf16[32,16,512]{0,1,2:T(8,128)(2,1)S(1)} %copy.17, bf16[64,32,512]{0,1,2:T(8,128)(2,1)} %copy.18), kind=kOutput, calls=%fused_computation.64 | convolution fusion | flops 33554432 | bytes 4718592 | tf_op jit(solution)/shard_map/quw,ugw->qgw/dot_general | solution.py:37
  122.0 1.2 fusion.38
  123.6 1.8 fusion.1
  125.8 2.2 %fusion = bf16[64,16,512]{0,1,2:T(8,128)(2,1)S(1)} fusion(f32[512,16,64]{2,1,0:T(8,128)S(1)} %fusion.37, f32[512]{0:T(512)S(1)} %broadcast_subtract_fusion, f32[512,16,64]{2,1,0:T(8,128)S(1)} %fusion.38, bf16[32,16,512]{0,1,2:T(8,128)(2,1)S(1)} %copy-done.3, bf16[64,32,512]{0,1,2:T(8,128)(2,1)S(1)} %copy-done.1, f32[512]{0:T(512)S(1)} %fusion.31), kind=kOutput, calls=%fused_computation.5 | convolution fusion | flops 36175872 | bytes 7868416 | tf_op jit(solution)/shard_map/quw,ugw->qgw/dot_general | solution.py:37
  128.0 2.8 %pad_maximum_fusion = bf16[64,16,1024]{0,1,2:T(8,128)(2,1)} fusion(bf16[64,16,512]{0,1,2:T(8,128)(2,1)S(1)} %fusion, bf16[64,16,512]{0,1,2:T(8,128)(2,1)S(1)} %fusion.1), kind=kLoop, calls=%fused_computation.1 | loop fusion | flops 1048576 | bytes 4194304 | tf_op jit(solution)/shard_map/concatenate | solution.py:45
  130.8 5.6 %copy.12 = bf16[64,16,1024]{2,0,1:T(8,128)(2,1)} copy(bf16[64,16,1024]{0,1,2:T(8,128)(2,1)} %pad_maximum_fusion) | data formatting | bytes 4194304 | tf_op jit(solution)/shard_map/concatenate | solution.py:45
  136.4 1.6 sort.17
  138.0 4.0 %multiply_convert_fusion = bf16[512,512]{1,0:T(8,128)(2,1)S(1)} fusion(f32[512]{0:T(512)S(1)} %select_multiply_fusion), kind=kLoop, calls=%fused_computation.24 | loop fusion | flops 4194304 | bytes 526336 | tf_op jit(solution)/shard_map/convert
  142.0 43.6 %reduce-scatter.2.cloned.1.call-done = bf16[64,2,1024]{2,0,1:T(8,128)(2,1)} async-done(((bf16[64,16,1024]{2,0,1:T(8,128)(2,1)}), bf16[64,2,1024]{2,0,1:T(8,128)(2,1)}) %reduce-scatter.2.cloned.1.call-update) | async-done | bytes 262160 | tf_op jit(solution)/shard_map/reduce_scatter | solution.py:77
  185.6 1.3 convolution_bitcast_fusion
  186.8 0.9 copy.13
  187.7 11.6 %all-to-all-start = ((f32[64,2,1,512]{3,1,2,0:T(2,128)}), f32[64,2,1,512]{3,1,2,0:T(2,128)S(1)}, u32[]{:S(2)}, u32[]{:S(2)}) async-start(f32[64,2,1,512]{3,1,2,0:T(2,128)} %copy.13), calls=%async_computation.1 | async-start | bytes 524288 | tf_op jit(solution)/shard_map/all_to_all | solution.py:86
  199.4 12.8 %all-to-all-done = f32[64,2,1,512]{3,1,2,0:T(2,128)S(1)} async-done(((f32[64,2,1,512]{3,1,2,0:T(2,128)}), f32[64,2,1,512]{3,1,2,0:T(2,128)S(1)}, u32[]{:S(2)}, u32[]{:S(2)}) %all-to-all-start) | async-done | bytes 262176 | tf_op jit(solution)/shard_map/all_to_all | solution.py:86
  (39 shorter events, 3.9 us)
Async XLA Ops:
  6.5 11.6 %copy-start = (bf16[32,16,1,256]{3,1,2,0:T(8,128)(2,1)S(1)}, bf16[32,16,1,256]{3,1,2,0:T(8,128)(2,1)}, u32[]{:S(2)}) copy-start(bf16[32,16,1,256]{3,1,2,0:T(8,128)(2,1)} %param.8) | copy-start | bytes 786436
  6.5 87.8 %all-gather.2.cloned.1.call-start = ((), (), s32[]{:S(2)}) async-start(), calls=%async_computation.2 | async-start | bytes 2162688 | tf_op jit(solution)/shard_map/all_gather | solution.py:72
  9.1 176.5 %reduce-scatter.2.cloned.1.call-start = ((), (), s32[]{:S(2)}) async-start(), calls=%async_computation.3 | async-start | bytes 2359296 | tf_op jit(solution)/shard_map/reduce_scatter | solution.py:77
  13.1 6.4 %copy-start.4 = (bf16[512,512]{1,0:T(8,128)(2,1)}, bf16[512,512]{1,0:T(8,128)(2,1)S(1)}, u32[]{:S(2)}) copy-start(bf16[512,512]{1,0:T(8,128)(2,1)S(1)} %fusion.19) | copy-start | bytes 1572868
  118.4 3.6 %copy-start.2 = (bf16[64,32,512]{0,1,2:T(8,128)(2,1)S(1)}, bf16[64,32,512]{0,1,2:T(8,128)(2,1)}, u32[]{:S(2)}) copy-start(bf16[64,32,512]{0,1,2:T(8,128)(2,1)} %copy.16) | copy-start | bytes 6291460
  122.0 1.6 copy-start.3
  123.6 2.2 copy-start.1
  130.8 5.6 %copy-start.8 = (s32[32]{0:T(128)S(1)}, s32[32]{0:T(128)}, u32[]{:S(2)}) copy-start(s32[32]{0:T(128)} %param.7) | copy-start | bytes 388
  130.8 54.8 %copy-start.6 = (bf16[512,512]{1,0:T(8,128)(2,1)S(1)}, bf16[512,512]{1,0:T(8,128)(2,1)}, u32[]{:S(2)}) copy-start(bf16[512,512]{1,0:T(8,128)(2,1)} %get-tuple-element.11) | copy-start | bytes 1572868
  136.3 76.8 %copy-start.5 = (f32[2,64,512]{2,1,0:T(8,128)S(1)}, f32[2,64,512]{2,1,0:T(8,128)}, u32[]{:S(2)}) copy-start(f32[2,64,512]{2,1,0:T(8,128)} %param.5) | copy-start | bytes 786436
  136.3 76.8 %copy-start.7 = (f32[2]{0:T(128)S(1)}, f32[2]{0:T(128)}, u32[]{:S(2)}) copy-start(f32[2]{0:T(128)} %param.9) | copy-start | bytes 28
  187.7 24.5 %all-to-all-start = ((f32[64,2,1,512]{3,1,2,0:T(2,128)}), f32[64,2,1,512]{3,1,2,0:T(2,128)S(1)}, u32[]{:S(2)}, u32[]{:S(2)}) async-start(f32[64,2,1,512]{3,1,2,0:T(2,128)} %copy.13), calls=%async_computation.1 | async-start | bytes 524288 | tf_op jit(solution)/shard_map/all_to_all | solution.py:86
Sparse Core Ops, SparseCore 0:
  10.1 84.1 all-gather.1
  136.5 49.0 reduce-scatter.1
where the time goes:
time: 221 us
  waiting for transfers between devices  124 us (56%)
  local copies, waits for them, and re-layouts  36.1 us (16%)
  other arithmetic  18.9 us (9%)
  matrix products  16.3 us (7%)
  between operations  13.6 us (6%)
  starting transfers between devices  11.6 us (5%)
    all_gather x1, waiting for transfers between devices, on_device(): piece_rows = lax.all_gather(gathered, 'shot', axis=0, tiled=True)  68 us
    reduce_scatter x1, waiting for transfers between devices, on_device(): lax.psum_scatter(partial_value.astype(jnp.bfloat16), 'surf', scatter_dime...  43.6 us
    unnamed x20, local copies, waits for them, and re-layouts  13.4 us
    another operation x3, other arithmetic  12.9 us
    all_to_all x1, waiting for transfers between devices, on_device(): lax.all_to_all(in_time, 'shot', split_axis=0, concat_axis=2, tiled=True)  12.8 us
    all_to_all x1, starting transfers between devices, on_device(): lax.all_to_all(in_time, 'shot', split_axis=0, concat_axis=2, tiled=True)  11.6 us
    slice x2, local copies, waits for them, and re-layouts, spectral_product(): left_real = left[..., :half]  11.3 us
    dot_general x4, matrix products, contract(): jnp.einsum('quw,ugw->qgw', leading_factor, trailing_factor, preferred_ele...  8.76 us
  transfers between devices with their start and end apart: 3, of which 3 were waited for; matrix products, arithmetic and copies ran while one was open for 10% of the time, Pallas kernels for 0%

commit v1 on v0

v1 whole, which is shorter than its diff:
```python
import math

import jax
import jax.numpy as jnp
import ml_dtypes
import numpy as np
from jax import lax
from jax.experimental import pallas as pl
from jax.experimental.pallas import tpu as pltpu

LANES = 128
NT_DIMS = (((1,), (1,)), ((), ()))


def fourier_tables(taps):
    length = 2 * taps
    frequency = np.arange(taps)[:, None]
    time = np.arange(length)[None, :]
    angle = (frequency * time % length) * (2.0 * math.pi / length)
    cosine, sine = np.cos(angle), np.sin(angle)
    alternate = 1.0 - 2.0 * (time % 2)
    packed = frequency == 0
    forward = np.concatenate([cosine, np.where(packed, alternate, -sine)], axis=0)
    weight = np.where(packed, 1.0, 2.0) / length
    inverse_real = (weight * cosine)[:, taps:]
    inverse_imag = np.where(packed, alternate / length, -2.0 * sine / length)[:, taps:]
    inverse = np.concatenate([inverse_real, inverse_imag], axis=1)
    return forward.astype(ml_dtypes.bfloat16), inverse.astype(ml_dtypes.bfloat16)


def exchange_groups(parts):
    lane = lax.broadcasted_iota(jnp.int32, parts[0].shape, 1)
    parts = list(parts)
    for bit in (1, 2):
        shift = bit * 32
        high = (lane & shift) != 0
        swapped = [None] * 4
        for low_index in range(4):
            if low_index & bit:
                continue
            low, top = parts[low_index], parts[low_index | bit]
            swapped[low_index] = jnp.where(high, pltpu.roll(top, shift, 1), low)
            swapped[low_index | bit] = jnp.where(high, top, pltpu.roll(low, LANES - shift, 1))
        parts = swapped
    return parts


def spectra_kernel(positions, data, primaries, forward, sent, rows, packed):
    shots, _, samples = data.shape
    position_count, width, taps = primaries.shape
    row_count = position_count * width
    frequencies = taps
    chunk = packed.shape[0] // frequencies
    groups = width // 4
    tap_table = forward[:, :taps]
    flat = primaries[...].reshape(row_count, taps)
    tiles = range(taps // LANES)
    for tile in tiles:
        rows[tile] = flat[:, tile * LANES : (tile + 1) * LANES].astype(jnp.float32)
    for group in range(groups):
        block = jnp.concatenate(
            [
                jnp.concatenate(
                    [rows[tile, pl.ds(4 * group + j, position_count, stride=width), :] for tile in tiles],
                    axis=1,
                )
                for j in range(4)
            ],
            axis=0,
        ).astype(jnp.bfloat16)
        spectra = lax.dot_general(tap_table, block, NT_DIMS, preferred_element_type=jnp.float32)
        for part in range(2):
            packed[pl.ds(part * groups + group, frequencies, stride=chunk), :] = spectra[
                part * frequencies : (part + 1) * frequencies
            ]
    place = lax.broadcasted_iota(jnp.int32, (position_count, positions.shape[1]), 0)
    onehot = (place == positions[...]).astype(jnp.float32)
    windows = []
    for shot in range(shots):
        gathered = jnp.dot(
            onehot, data[shot], precision=lax.Precision.HIGHEST, preferred_element_type=jnp.float32
        ).astype(jnp.bfloat16)
        before = jnp.zeros((position_count, taps), jnp.bfloat16)
        windows.append(jnp.concatenate([before, gathered[:, :taps]], axis=1))
        windows.append(gathered)
    window = jnp.concatenate(windows, axis=0)
    spectra = lax.dot_general(forward[...], window, NT_DIMS, preferred_element_type=jnp.float32)
    for part in range(2):
        packed[pl.ds(2 * groups + part, frequencies, stride=chunk), :] = spectra[
            part * frequencies : (part + 1) * frequencies
        ]
    sent[...] = packed[...].astype(jnp.bfloat16)


def product_kernel(shot_devices, surf_devices, width, received, sent, rows, packed):
    rows[...] = received[...].astype(jnp.float32)
    chunk = received.shape[0] // (shot_devices * surf_devices)
    groups = width // 4

    def regrouped(row):
        halves = []
        for half in range(surf_devices // 4):
            parts = [
                rows[pl.ds((half * 4 + i) * chunk + row, shot_devices, stride=surf_devices * chunk), :]
                for i in range(4)
            ]
            halves.append(exchange_groups(parts))
        return [
            jnp.concatenate([half[j] for half in halves], axis=1).astype(jnp.bfloat16) for j in range(4)
        ]

    primary = []
    for part in range(2):
        by_receiver = []
        for group in range(groups):
            by_receiver += regrouped(part * groups + group)
        primary.append(by_receiver)
    traces = [jnp.concatenate(regrouped(2 * groups + part), axis=0) for part in range(2)]
    frequency = lax.axis_index("shot") * surf_devices + lax.axis_index("surf")
    interior = frequency > 0
    pair = width // surf_devices
    for block in range(surf_devices):
        which = range(pair * block, pair * (block + 1))
        real = jnp.concatenate([primary[0][q] for q in which], axis=0)
        imag = jnp.concatenate([primary[1][q] for q in which], axis=0)
        none = jnp.zeros_like(imag)
        with_real = jnp.concatenate([real, jnp.where(interior, imag, none)], axis=0)
        with_imag = jnp.concatenate(
            [jnp.where(interior, -imag, none), jnp.where(interior, real, imag)], axis=0
        )
        product = lax.dot_general(
            traces[0], with_real, NT_DIMS, preferred_element_type=jnp.float32
        ) + lax.dot_general(traces[1], with_imag, NT_DIMS, preferred_element_type=jnp.float32)
        for window in range(4):
            packed[pl.ds(block * 4 + window, shot_devices, stride=surf_devices * 4), :] = product[
                window * shot_devices : (window + 1) * shot_devices
            ]
    sent[...] = packed[...].astype(jnp.bfloat16)


def subtract_kernel(place, scale, received, inverse, data, out, rows):
    shots, receivers, _ = data.shape
    frequencies, columns = inverse.shape
    taps = columns // 2
    windows = received.shape[0] // frequencies
    rows[...] = received[...].astype(jnp.float32)
    order = (lax.broadcasted_iota(jnp.int32, (LANES, LANES), 0) == place[...]).astype(jnp.bfloat16)
    for window in range(windows):
        spectra = rows[pl.ds(window, frequencies, stride=windows), :].astype(jnp.bfloat16)
        turned = lax.dot_general(order, spectra, NT_DIMS, preferred_element_type=jnp.float32).astype(
            jnp.bfloat16
        )
        in_time = jnp.dot(
            turned[:receivers], inverse[:, :taps], preferred_element_type=jnp.float32
        ) + jnp.dot(turned[receivers:], inverse[:, taps:], preferred_element_type=jnp.float32)
        shot, half = divmod(window, windows // shots)
        span = slice(half * taps, (half + 1) * taps)
        out[shot, :, span] = data[shot, :, span] - scale[shot] * in_time


def on_device(shot_devices, surf_devices, data, positions, plan, primaries, scale):
    shots, receivers, samples = data.shape
    position_count, width, _, taps = primaries.shape
    devices = shot_devices * surf_devices
    forward, inverse = fourier_tables(taps)
    forward, inverse = jnp.asarray(forward), jnp.asarray(inverse)
    local = (positions - lax.axis_index("surf") * position_count).reshape(1, receivers)
    chunk = (2 * width * position_count + 2 * 2 * shots * position_count) // LANES
    vmem = pl.BlockSpec(memory_space=pltpu.VMEM)
    smem = pl.BlockSpec(memory_space=pltpu.SMEM)
    limit = pltpu.CompilerParams(vmem_limit_bytes=32 * 1024 * 1024)

    sent = pl.pallas_call(
        spectra_kernel,
        out_shape=jax.ShapeDtypeStruct((taps * chunk, LANES), jnp.bfloat16),
        in_specs=[vmem] * 4,
        out_specs=vmem,
        scratch_shapes=[
            pltpu.VMEM((taps // LANES, position_count * width, LANES), jnp.float32),
            pltpu.VMEM((taps * chunk, LANES), jnp.float32),
        ],
        compiler_params=limit,
    )(local, data, primaries.reshape(position_count, width, taps), forward)
    sent = sent.reshape(devices, chunk // 2, 2, LANES)
    received = lax.all_to_all(sent, ("shot", "surf"), 0, 0, tiled=True)
    received = received.reshape(devices * chunk, LANES)

    back = devices * 4

    def product(*refs):
        product_kernel(shot_devices, surf_devices, width, *refs)

    terms = pl.pallas_call(
        product,
        out_shape=jax.ShapeDtypeStruct((back, LANES), jnp.bfloat16),
        in_specs=[vmem],
        out_specs=vmem,
        scratch_shapes=[
            pltpu.VMEM((devices * chunk, LANES), jnp.float32),
            pltpu.VMEM((back, LANES), jnp.float32),
        ],
        compiler_params=limit,
    )(received)
    terms = lax.all_to_all(terms.reshape(devices, 4, LANES), ("shot", "surf"), 0, 0, tiled=True)
    terms = terms.reshape(back, LANES)

    pair = width // surf_devices
    offset = jnp.arange(2 * pair, dtype=jnp.int32) * plan.shape[0]
    place = (offset[:, None] + plan[None, :]).reshape(1, LANES)
    return pl.pallas_call(
        subtract_kernel,
        out_shape=jax.ShapeDtypeStruct(data.shape, jnp.float32),
        in_specs=[vmem, smem, vmem, vmem, vmem],
        out_specs=vmem,
        scratch_shapes=[pltpu.VMEM((back, LANES), jnp.float32)],
        compiler_params=limit,
    )(place, scale, terms, inverse, data)


def solution(mesh):
    P = jax.sharding.PartitionSpec
    shot_devices, surf_devices = mesh.shape["shot"], mesh.shape["surf"]

    def device(*args):
        return on_device(shot_devices, surf_devices, *args)

    in_specs = (P("shot", "surf", None), P("surf"), P(), P("surf", None, "shot", None), P("shot"))
    out_specs = P("shot", "surf", None)
    return jax.shard_map(device, mesh=mesh, in_specs=in_specs, out_specs=out_specs, check_vma=False)
```

time: 221 us -> 69.1 us (0.31)
  waiting for transfers between devices: 124 us -> 14.5 us
  blocking collectives: 0 us -> 39.7 us
  local copies, waits for them, and re-layouts: 36.1 us -> 4.33 us
  other arithmetic: 18.9 us -> 0.08 us
  matrix products: 16.3 us -> 0 us
  between operations: 13.6 us -> 0.05 us
  starting transfers between devices: 11.6 us -> 5.3 us
  Pallas kernels: 0 us -> 4.88 us
    all_gather x1 -> x0, waiting for transfers between devices: 68 us -> none  [on_device(): piece_rows = lax.all_gather(gathered, 'shot', axis=0, tiled=True)]
    reduce_scatter x1 -> x0, waiting for transfers between devices: 43.6 us -> none  [on_device(): lax.psum_scatter(partial_value.astype(jnp.bfloat16), 'surf', scatter_dime...]
    all_to_all x0 -> x1, blocking collectives: none -> 39.7 us  [on_device(): received = lax.all_to_all(sent, ('shot', 'surf'), 0, 0, tiled=True)]
    dot_general x8 -> x0, matrix products: 16.3 us -> none  [the longest x4 8.76 us: contract(): jnp.einsum('quw,ugw->qgw', leading_factor, trailing_factor, preferred_ele...]
    slice x4 -> x0, local copies, waits for them, and re-layouts: 15.2 us -> none  [the longest x2 11.3 us: spectral_product(): left_real = left[..., :half]]
    another operation x3 -> x0, other arithmetic: 12.9 us -> none
    unnamed x20 -> x16, local copies, waits for them, and re-layouts: 13.4 us -> 4.25 us
    all_to_all x1, starting transfers between devices: 11.6 us -> 5.3 us  [on_device(): lax.all_to_all(terms.reshape(devices, 4, LANES), ('shot', 'surf'), 0, 0,...]
  transfers between devices with their start and end apart: 3 -> 1, of which waited for: 3 -> 1; matrix products, arithmetic and copies ran while one was open for 10% -> 0% of each run, Pallas kernels for 0% -> 0%
where the time goes in v1:
time: 69.1 us; the launch traced here: 68.8 us
  blocking collectives  39.7 us (57%)
  waiting for transfers between devices  14.5 us (21%)
  starting transfers between devices  5.3 us (8%)
  Pallas kernels  4.88 us (7%)
  local copies, waits for them, and re-layouts  4.33 us (6%)
    all_to_all x1, blocking collectives, on_device(): received = lax.all_to_all(sent, ('shot', 'surf'), 0, 0, tiled=True)  39.7 us
    all_to_all x1, waiting for transfers between devices, on_device(): lax.all_to_all(terms.reshape(devices, 4, LANES), ('shot', 'surf'), 0, 0,...  14.5 us
    all_to_all x1, starting transfers between devices, on_device(): lax.all_to_all(terms.reshape(devices, 4, LANES), ('shot', 'surf'), 0, 0,...  5.3 us
    unnamed x16, local copies, waits for them, and re-layouts  4.25 us
    pallas_call x1, Pallas kernels, on_device(): pl.pallas_call(product, out_shape=jax.ShapeDtypeStruct((back, LANES), jnp...  1.96 us
    pallas_call x1, Pallas kernels, on_device(): pl.pallas_call(subtract_kernel, out_shape=jax.ShapeDtypeStruct(data.shape...  1.86 us
  transfers between devices with their start and end apart: 1, of which 1 were waited for; matrix products, arithmetic and copies ran while one was open for 0% of the time, Pallas kernels for 0%

profile of v1, /device:TPU:1, one launch (start us, length us, event | category | flops | bytes accessed | tf_op | source)
XLA Modules:
  0.0 68.8 jit_solution(15732369815477586990)
XLA Ops:
  0.0 0.0 copy-start.7
  0.0 0.7 copy-done.7
  0.7 0.0 copy-start
  0.7 0.9 %copy-done = f32[2,64,512]{2,1,0:T(8,128)S(1)} copy-done((f32[2,64,512]{2,1,0:T(8,128)S(1)}, f32[2,64,512]{2,1,0:T(8,128)}, u32[]{:S(2)}) %copy-start) | copy-done | bytes 262168
  1.6 0.0 copy-start.2
  1.6 1.0 %copy-done.2 = bf16[512,512]{1,0:T(8,128)(2,1)S(1)} copy-done((bf16[512,512]{1,0:T(8,128)(2,1)S(1)}, bf16[512,512]{1,0:T(8,128)(2,1)}, u32[]{:S(2)}) %copy-start.2) | copy-done | bytes 524312
  2.7 0.0 copy-start.3
  2.7 0.9 %copy-done.3 = bf16[32,16,1,256]{3,1,2,0:T(8,128)(2,1)S(1)} copy-done((bf16[32,16,1,256]{3,1,2,0:T(8,128)(2,1)S(1)}, bf16[32,16,1,256]{3,1,2,0:T(8,128)(2,1)}, u32[]{:S(2)}) %copy-start.3) | copy-done | bytes 262168
  3.6 1.1 %shard_map.73 = bf16[2560,128]{1,0:T(8,128)(2,1)S(1)} custom-call(s32[1,64]{1,0:T(1,128)S(1)} %subtract_bitcast_fusion.positions, f32[2,64,512]{2,1,0:T(8,128)S(1)} %copy-done, bf16[32,16,256]{2,1,0:T(8,128)(2,1)S(1)} %bitcast.10, bf16[512,512]{1,0:T(8,128)(2,1)S(1)} %copy-done.2), custom_call_target="tpu_custom_call" | custom-call | tf_op jit(solution)/shard_map/pallas_call | solution.py:173
  4.7 39.7 %all_to_all.10 = bf16[256,5,2,128]{3,2,1,0:T(2,128)(2,1)S(1)} all-to-all(bf16[256,5,2,128]{3,2,1,0:T(2,128)(2,1)S(1)} %bitcast.7), channel_id=1, replica_groups=mesh['shot'=32,'surf'=8] {'shot','surf'}, dimensions={0} | all-to-all | bytes 1310720 | tf_op jit(solution)/shard_map/all_to_all | solution.py:185
  44.4 2.0 %shard_map.74 = bf16[1024,128]{1,0:T(8,128)(2,1)} custom-call(bf16[2560,128]{1,0:T(8,128)(2,1)S(1)} %bitcast.8), custom_call_target="tpu_custom_call" | custom-call | tf_op jit(solution)/shard_map/pallas_call | solution.py:193
  46.3 0.0 copy-start.1
  46.3 0.0 copy-start.4
  46.3 5.3 %all-to-all-start.1 = ((bf16[256,4,128]{2,1,0:T(4,128)(2,1)}), bf16[256,4,128]{2,1,0:T(4,128)(2,1)S(1)}, u32[]{:S(2)}, u32[]{:S(2)}) async-start(bf16[256,4,128]{2,1,0:T(4,128)(2,1)} %bitcast.4), calls=%async_computation.1 | async-start | bytes 524288 | tf_op jit(solution)/shard_map/all_to_all | solution.py:204
  51.7 0.0 copy-start.6
  51.7 0.6 copy-done.6
  52.3 0.1 broadcast_add_fusion
  52.4 0.1 add.26.place
  52.5 0.0 copy-start.5
  52.5 14.5 %all-to-all-done.1 = bf16[256,4,128]{2,1,0:T(4,128)(2,1)S(1)} async-done(((bf16[256,4,128]{2,1,0:T(4,128)(2,1)}), bf16[256,4,128]{2,1,0:T(4,128)(2,1)S(1)}, u32[]{:S(2)}, u32[]{:S(2)}) %all-to-all-start.1) | async-done | bytes 262176 | tf_op jit(solution)/shard_map/all_to_all | solution.py:204
  67.0 0.0 copy-done.1
  67.0 0.0 copy-done.4
  67.0 0.0 copy-done.5
  67.0 1.9 %shard_map.75 = f32[2,64,512]{2,1,0:T(8,128)} custom-call(s32[1,128]{1,0:T(1,128)S(1)} %add.26.place, f32[2]{0:T(128)S(1)} %copy-done.5, bf16[1024,128]{1,0:T(8,128)(2,1)S(1)} %bitcast.9, bf16[256,512]{1,0:T(8,128)(2,1)S(1)} %copy-done.4, f32[2,64,512]{2,1,0:T(8,128)S(1)} %copy-done.1), custom_call_target="tpu_custom_call" | custom-call | tf_op jit(solution)/shard_map/pallas_call | solution.py:210
  (2 shorter events, 0.0 us)
Async XLA Ops:
  0.0 0.7 copy-start.7
  0.7 0.9 %copy-start = (f32[2,64,512]{2,1,0:T(8,128)S(1)}, f32[2,64,512]{2,1,0:T(8,128)}, u32[]{:S(2)}) copy-start(f32[2,64,512]{2,1,0:T(8,128)} %data.3) | copy-start | bytes 786436
  1.6 1.0 %copy-start.2 = (bf16[512,512]{1,0:T(8,128)(2,1)S(1)}, bf16[512,512]{1,0:T(8,128)(2,1)}, u32[]{:S(2)}) copy-start(bf16[512,512]{1,0:T(8,128)(2,1)} %constant.3.clone.forward) | copy-start | bytes 1572868
  2.7 0.9 %copy-start.3 = (bf16[32,16,1,256]{3,1,2,0:T(8,128)(2,1)S(1)}, bf16[32,16,1,256]{3,1,2,0:T(8,128)(2,1)}, u32[]{:S(2)}) copy-start(bf16[32,16,1,256]{3,1,2,0:T(8,128)(2,1)} %param.10) | copy-start | bytes 786436
  46.3 20.6 %copy-start.1 = (f32[2,64,512]{2,1,0:T(8,128)S(1)}, f32[2,64,512]{2,1,0:T(8,128)}, u32[]{:S(2)}) copy-start(f32[2,64,512]{2,1,0:T(8,128)} %data.3) | copy-start | bytes 786436
  46.3 20.6 %copy-start.4 = (bf16[256,512]{1,0:T(8,128)(2,1)S(1)}, bf16[256,512]{1,0:T(8,128)(2,1)}, u32[]{:S(2)}) copy-start(bf16[256,512]{1,0:T(8,128)(2,1)} %constant.12.clone.inverse) | copy-start | bytes 786436
  46.3 20.6 %all-to-all-start.1 = ((bf16[256,4,128]{2,1,0:T(4,128)(2,1)}), bf16[256,4,128]{2,1,0:T(4,128)(2,1)S(1)}, u32[]{:S(2)}, u32[]{:S(2)}) async-start(bf16[256,4,128]{2,1,0:T(4,128)(2,1)} %bitcast.4), calls=%async_computation.1 | async-start | bytes 524288 | tf_op jit(solution)/shard_map/all_to_all | solution.py:204
  51.7 0.7 copy-start.6
  52.5 14.5 %copy-start.5 = (f32[2]{0:T(128)S(1)}, f32[2]{0:T(128)}, u32[]{:S(2)}) copy-start(f32[2]{0:T(128)} %scale.1) | copy-start | bytes 28

commit v2 on v1

--- a/solution.py
+++ b/solution.py
@@ -20,11 +20,11 @@
     cosine, sine = np.cos(angle), np.sin(angle)
     alternate = 1.0 - 2.0 * (time % 2)
     packed = frequency == 0
-    forward = np.concatenate([cosine, np.where(packed, alternate, -sine)], axis=0)
+    forward = np.concatenate([cosine, np.where(packed, alternate, -sine)], axis=0)[:, :taps]
     weight = np.where(packed, 1.0, 2.0) / length
     inverse_real = (weight * cosine)[:, taps:]
     inverse_imag = np.where(packed, alternate / length, -2.0 * sine / length)[:, taps:]
-    inverse = np.concatenate([inverse_real, inverse_imag], axis=1)
+    inverse = np.concatenate([inverse_real, inverse_imag], axis=0)
     return forward.astype(ml_dtypes.bfloat16), inverse.astype(ml_dtypes.bfloat16)
 
 
@@ -45,18 +45,51 @@
     return parts
 
 
-def spectra_kernel(positions, data, primaries, forward, sent, rows, packed):
+def spectra_kernel(
+    positions_in,
+    plan_in,
+    scale_in,
+    data_in,
+    primaries_in,
+    forward_in,
+    sent,
+    place,
+    gain,
+    positions,
+    plan,
+    scale,
+    data,
+    primaries,
+    forward,
+    rows,
+    packed,
+    arrived,
+):
     shots, _, samples = data.shape
     position_count, width, taps = primaries.shape
     row_count = position_count * width
     frequencies = taps
     chunk = packed.shape[0] // frequencies
     groups = width // 4
-    tap_table = forward[:, :taps]
+
+    def halves(far, near):
+        half = far.shape[0] // 2
+        return [(far.at[pl.ds(i * half, half)], near.at[pl.ds(i * half, half)]) for i in range(2)]
+
+    pairs = halves(primaries_in, primaries) + halves(forward_in, forward) + halves(data_in, data)
+    pairs += [(positions_in, positions), (plan_in, plan), (scale_in, scale)]
+    copies = [pltpu.make_async_copy(far, near, arrived.at[i]) for i, (far, near) in enumerate(pairs)]
+    for copy in copies:
+        copy.start()
+
+    for copy in copies[:2]:
+        copy.wait()
     flat = primaries[...].reshape(row_count, taps)
     tiles = range(taps // LANES)
     for tile in tiles:
         rows[tile] = flat[:, tile * LANES : (tile + 1) * LANES].astype(jnp.float32)
+    for copy in copies[2:4]:
+        copy.wait()
     for group in range(groups):
         block = jnp.concatenate(
             [
@@ -68,23 +101,33 @@
             ],
             axis=0,
         ).astype(jnp.bfloat16)
-        spectra = lax.dot_general(tap_table, block, NT_DIMS, preferred_element_type=jnp.float32)
+        spectra = lax.dot_general(forward[...], block, NT_DIMS, preferred_element_type=jnp.float32)
         for part in range(2):
             packed[pl.ds(part * groups + group, frequencies, stride=chunk), :] = spectra[
                 part * frequencies : (part + 1) * frequencies
             ]
-    place = lax.broadcasted_iota(jnp.int32, (position_count, positions.shape[1]), 0)
-    onehot = (place == positions[...]).astype(jnp.float32)
-    windows = []
+
+    for copy in copies[4:]:
+        copy.wait()
+    place[...] = jnp.concatenate([plan[...] + i * plan.shape[1] for i in range(4)], axis=1)
+    for shot in range(shots):
+        gain[pl.ds(shot, 1), :] = jnp.full((1, taps), scale[shot], jnp.float32)
+    first = lax.axis_index("surf") * position_count
+    position = lax.broadcasted_iota(jnp.int32, (position_count, positions.shape[1]), 0) + first
+    onehot = (position == positions[...]).astype(jnp.float32)
+    halves_in_time = []
     for shot in range(shots):
         gathered = jnp.dot(
             onehot, data[shot], precision=lax.Precision.HIGHEST, preferred_element_type=jnp.float32
         ).astype(jnp.bfloat16)
-        before = jnp.zeros((position_count, taps), jnp.bfloat16)
-        windows.append(jnp.concatenate([before, gathered[:, :taps]], axis=1))
-        windows.append(gathered)
-    window = jnp.concatenate(windows, axis=0)
-    spectra = lax.dot_general(forward[...], window, NT_DIMS, preferred_element_type=jnp.float32)
+        halves_in_time += [gathered[:, :taps], gathered[:, taps:]]
+    spectra = lax.dot_general(
+        forward[...], jnp.concatenate(halves_in_time, axis=0), NT_DIMS, preferred_element_type=jnp.float32
+    )
+    odd = lax.broadcasted_iota(jnp.int32, spectra.shape, 0) % 2 == 1
+    second = lax.broadcasted_iota(jnp.int32, spectra.shape, 1) % (2 * position_count) >= position_count
+    earlier = jnp.where(second, pltpu.roll(spectra, position_count, 1), 0.0)
+    spectra = earlier + jnp.where(odd, -spectra, spectra)
     for part in range(2):
         packed[pl.ds(2 * groups + part, frequencies, stride=chunk), :] = spectra[
             part * frequencies : (part + 1) * frequencies
@@ -101,13 +144,13 @@
         halves = []
         for half in range(surf_devices // 4):
             parts = [
-                rows[pl.ds((half * 4 + i) * chunk + row, shot_devices, stride=surf_devices * chunk), :]
+                rows[pl.ds((half * 4 + i) * chunk + row, shot_devices, stride=surf_devices * chunk), :].astype(
+                    jnp.bfloat16
+                )
                 for i in range(4)
             ]
             halves.append(exchange_groups(parts))
-        return [
-            jnp.concatenate([half[j] for half in halves], axis=1).astype(jnp.bfloat16) for j in range(4)
-        ]
+        return [jnp.concatenate([half[j] for half in halves], axis=1) for j in range(4)]
 
     primary = []
     for part in range(2):
@@ -138,24 +181,39 @@
     sent[...] = packed[...].astype(jnp.bfloat16)
 
 
-def subtract_kernel(place, scale, received, inverse, data, out, rows):
+def subtract_kernel(place, gain, received, inverse, data, out, rows, result, written):
     shots, receivers, _ = data.shape
-    frequencies, columns = inverse.shape
-    taps = columns // 2
+    frequencies, taps = inverse.shape[0] // 2, inverse.shape[1]
     windows = received.shape[0] // frequencies
     rows[...] = received[...].astype(jnp.float32)
     order = (lax.broadcasted_iota(jnp.int32, (LANES, LANES), 0) == place[...]).astype(jnp.bfloat16)
-    for window in range(windows):
-        spectra = rows[pl.ds(window, frequencies, stride=windows), :].astype(jnp.bfloat16)
+    copies = []
+    for shot in range(shots):
+        spectra = jnp.concatenate(
+            [
+                rows[pl.ds(window, frequencies, stride=windows), :].astype(jnp.bfloat16)
+                for window in (2 * shot, 2 * shot + 1)
+            ],
+            axis=0,
+        )
         turned = lax.dot_general(order, spectra, NT_DIMS, preferred_element_type=jnp.float32).astype(
             jnp.bfloat16
         )
-        in_time = jnp.dot(
-            turned[:receivers], inverse[:, :taps], preferred_element_type=jnp.float32
-        ) + jnp.dot(turned[receivers:], inverse[:, taps:], preferred_element_type=jnp.float32)
-        shot, half = divmod(window, windows // shots)
-        span = slice(half * taps, (half + 1) * taps)
-        out[shot, :, span] = data[shot, :, span] - scale[shot] * in_time
+        spans = [slice(half * frequencies, (half + 1) * frequencies) for half in range(2)]
+        turned = jnp.concatenate(
+            [jnp.concatenate([turned[:receivers, span], turned[receivers:, span]], axis=1) for span in spans],
+            axis=0,
+        )
+        in_time = jnp.dot(turned, inverse[...], preferred_element_type=jnp.float32)
+        for half in range(2):
+            span = slice(half * taps, (half + 1) * taps)
+            result[shot, :, span] = (
+                data[shot, :, span] - gain[pl.ds(shot, 1), :] * in_time[half * receivers : (half + 1) * receivers]
+            )
+        copies.append(pltpu.make_async_copy(result.at[shot], out.at[shot], written.at[shot]))
+        copies[-1].start()
+    for copy in copies:
+        copy.wait()
 
 
 def on_device(shot_devices, surf_devices, data, positions, plan, primaries, scale):
@@ -164,23 +222,45 @@
     devices = shot_devices * surf_devices
     forward, inverse = fourier_tables(taps)
     forward, inverse = jnp.asarray(forward), jnp.asarray(inverse)
-    local = (positions - lax.axis_index("surf") * position_count).reshape(1, receivers)
     chunk = (2 * width * position_count + 2 * 2 * shots * position_count) // LANES
     vmem = pl.BlockSpec(memory_space=pltpu.VMEM)
-    smem = pl.BlockSpec(memory_space=pltpu.SMEM)
+    hbm = pl.BlockSpec(memory_space=pltpu.HBM)
     limit = pltpu.CompilerParams(vmem_limit_bytes=32 * 1024 * 1024)
 
-    sent = pl.pallas_call(
+    sent, place, gain = pl.pallas_call(
         spectra_kernel,
-        out_shape=jax.ShapeDtypeStruct((taps * chunk, LANES), jnp.bfloat16),
-        in_specs=[vmem] * 4,
-        out_specs=vmem,
+        out_shape=(
+            jax.ShapeDtypeStruct((taps * chunk, LANES), jnp.bfloat16),
+            jax.ShapeDtypeStruct((1, LANES), jnp.int32),
+            jax.ShapeDtypeStruct((shots, taps), jnp.float32),
+        ),
+        in_specs=[hbm] * 6,
+        out_specs=(vmem, vmem, vmem),
         scratch_shapes=[
+            pltpu.VMEM((1, receivers), jnp.int32),
+            pltpu.VMEM((1, plan.shape[0]), jnp.int32),
+            pltpu.SMEM((shots,), jnp.float32),
+            pltpu.VMEM(data.shape, jnp.float32),
+            pltpu.VMEM((position_count, width, taps), jnp.bfloat16),
+            pltpu.VMEM(forward.shape, jnp.bfloat16),
             pltpu.VMEM((taps // LANES, position_count * width, LANES), jnp.float32),
             pltpu.VMEM((taps * chunk, LANES), jnp.float32),
+            pltpu.SemaphoreType.DMA((9,)),
         ],
         compiler_params=limit,
-    )(local, data, primaries.reshape(position_count, width, taps), forward)
+    )(
+        *(
+            pltpu.with_memory_space_constraint(operand, pltpu.HBM)
+            for operand in (
+                positions.reshape(1, receivers),
+                plan.reshape(1, plan.shape[0]),
+                scale,
+                data,
+                primaries.reshape(position_count, width, taps),
+                forward,
+            )
+        )
+    )
     sent = sent.reshape(devices, chunk // 2, 2, LANES)
     received = lax.all_to_all(sent, ("shot", "surf"), 0, 0, tiled=True)
     received = received.reshape(devices * chunk, LANES)
@@ -204,17 +284,18 @@
     terms = lax.all_to_all(terms.reshape(devices, 4, LANES), ("shot", "surf"), 0, 0, tiled=True)
     terms = terms.reshape(back, LANES)
 
-    pair = width // surf_devices
-    offset = jnp.arange(2 * pair, dtype=jnp.int32) * plan.shape[0]
-    place = (offset[:, None] + plan[None, :]).reshape(1, LANES)
     return pl.pallas_call(
         subtract_kernel,
         out_shape=jax.ShapeDtypeStruct(data.shape, jnp.float32),
-        in_specs=[vmem, smem, vmem, vmem, vmem],
-        out_specs=vmem,
-        scratch_shapes=[pltpu.VMEM((back, LANES), jnp.float32)],
+        in_specs=[vmem] * 5,
+        out_specs=hbm,
+        scratch_shapes=[
+            pltpu.VMEM((back, LANES), jnp.float32),
+            pltpu.VMEM(data.shape, jnp.float32),
+            pltpu.SemaphoreType.DMA((shots,)),
+        ],
         compiler_params=limit,
-    )(place, scale, terms, inverse, data)
+    )(place, gain, terms, inverse, data)
 
 
 def solution(mesh):

time: 69.1 us -> 64.9 us (0.939)
  blocking collectives: 39.7 us -> 60.2 us
  waiting for transfers between devices: 14.5 us -> 0 us
  starting transfers between devices: 5.3 us -> 0 us
  local copies, waits for them, and re-layouts: 4.33 us -> 0.01 us
    all_to_all x0 -> x1, blocking collectives: none -> 20.4 us  [on_device(): lax.all_to_all(terms.reshape(devices, 4, LANES), ('shot', 'surf'), 0, 0,...]
    all_to_all x1 -> x0, waiting for transfers between devices: 14.5 us -> none  [on_device(): lax.all_to_all(terms.reshape(devices, 4, LANES), ('shot', 'surf'), 0, 0,...]
    all_to_all x1 -> x0, starting transfers between devices: 5.3 us -> none  [on_device(): lax.all_to_all(terms.reshape(devices, 4, LANES), ('shot', 'surf'), 0, 0,...]
    unnamed x16 -> x4, local copies, waits for them, and re-layouts: 4.25 us -> 0.01 us
    pallas_call x1, Pallas kernels: 1.06 us -> 2.31 us  [on_device(): pl.pallas_call(spectra_kernel, out_shape=(jax.ShapeDtypeStruct((taps * ch...]
    pallas_call x1, Pallas kernels: 1.96 us -> 1.14 us  [on_device(): pl.pallas_call(product, out_shape=jax.ShapeDtypeStruct((back, LANES), jnp...]
    pallas_call x1, Pallas kernels: 1.86 us -> 1.12 us  [on_device(): pl.pallas_call(subtract_kernel, out_shape=jax.ShapeDtypeStruct(data.shape...]
  transfers between devices with their start and end apart: 1 -> 0, of which waited for: 1 -> 0; matrix products, arithmetic and copies ran while one was open for 0% -> 0% of each run, Pallas kernels for 0% -> 0%
where the time goes in v2:
time: 64.9 us; the launch traced here: 64.8 us
  blocking collectives  60.2 us (93%)
  Pallas kernels  4.58 us (7%)
    all_to_all x1, blocking collectives, on_device(): received = lax.all_to_all(sent, ('shot', 'surf'), 0, 0, tiled=True)  39.7 us
    all_to_all x1, blocking collectives, on_device(): lax.all_to_all(terms.reshape(devices, 4, LANES), ('shot', 'surf'), 0, 0,...  20.4 us
    pallas_call x1, Pallas kernels, on_device(): pl.pallas_call(spectra_kernel, out_shape=(jax.ShapeDtypeStruct((taps * ch...  2.31 us

profile of v2, /device:TPU:1, one launch (start us, length us, event | category | flops | bytes accessed | tf_op | source)
XLA Modules:
  0.0 64.8 jit_solution(12771864249607499729)
XLA Ops:
  0.0 2.3 %shard_map.73 = (bf16[2560,128]{1,0:T(8,128)(2,1)S(1)}, s32[1,128]{1,0:T(1,128)S(1)}, f32[2,256]{1,0:T(2,128)S(1)}) custom-call(s32[1,64]{1,0:T(1,128)} %bitcast.12, s32[1,32]{1,0:T(1,128)} %bitcast.13, f32[2]{0:T(128)} %scale_in.1, f32[2,64,512]{2,1,0:T(8,128)} %data.1, bf16[32,16,256]{2,1,0:T(8,128)(2,1)} %bitcast.11, ...), custom_call_target="tpu_custom_call" | custom-call | tf_op jit(solution)/shard_map/pallas_call | solution.py:230
  2.3 39.7 %all_to_all.10 = bf16[256,5,2,128]{3,2,1,0:T(2,128)(2,1)S(1)} all-to-all(bf16[256,5,2,128]{3,2,1,0:T(2,128)(2,1)S(1)} %bitcast.10), channel_id=1, replica_groups=mesh['shot'=32,'surf'=8] {'shot','surf'}, dimensions={0} | all-to-all | bytes 1310720 | tf_op jit(solution)/shard_map/all_to_all | solution.py:265
  42.0 1.1 %shard_map.74 = bf16[1024,128]{1,0:T(8,128)(2,1)S(1)} custom-call(bf16[2560,128]{1,0:T(8,128)(2,1)S(1)} %bitcast.7), custom_call_target="tpu_custom_call" | custom-call | tf_op jit(solution)/shard_map/pallas_call | solution.py:273
  43.2 0.0 copy-start
  43.2 0.0 copy-start.1
  43.2 20.4 %all_to_all.11 = bf16[256,4,128]{2,1,0:T(4,128)(2,1)S(1)} all-to-all(bf16[256,4,128]{2,1,0:T(4,128)(2,1)S(1)} %bitcast.8), channel_id=1, replica_groups=mesh['shot'=32,'surf'=8] {'shot','surf'}, dimensions={0} | all-to-all | bytes 524288 | tf_op jit(solution)/shard_map/all_to_all | solution.py:284
  63.7 0.0 copy-done
  63.7 0.0 copy-done.1
  63.7 1.1 %shard_map.75 = f32[2,64,512]{2,1,0:T(8,128)} custom-call(s32[1,128]{1,0:T(1,128)S(1)} %get-tuple-element.8.place, f32[2,256]{1,0:T(2,128)S(1)} %get-tuple-element.9.gain, bf16[1024,128]{1,0:T(8,128)(2,1)S(1)} %bitcast.9, bf16[512,256]{1,0:T(8,128)(2,1)S(1)} %copy-done.1, f32[2,64,512]{2,1,0:T(8,128)S(1)} %copy-done), custom_call_target="tpu_custom_call" | custom-call | tf_op jit(solution)/shard_map/pallas_call | solution.py:287
Async XLA Ops:
  43.2 20.5 %copy-start = (f32[2,64,512]{2,1,0:T(8,128)S(1)}, f32[2,64,512]{2,1,0:T(8,128)}, u32[]{:S(2)}) copy-start(f32[2,64,512]{2,1,0:T(8,128)} %data.1) | copy-start | bytes 786436
  43.2 20.5 %copy-start.1 = (bf16[512,256]{1,0:T(8,128)(2,1)S(1)}, bf16[512,256]{1,0:T(8,128)(2,1)}, u32[]{:S(2)}) copy-start(bf16[512,256]{1,0:T(8,128)(2,1)} %constant.5.clone.inverse) | copy-start | bytes 786436

commit v3 on v2

--- a/solution.py
+++ b/solution.py
@@ -9,7 +9,26 @@
 from jax.experimental.pallas import tpu as pltpu
 
 LANES = 128
+SHOT = ("z2", "z1", "z0", "yh", "core")
+SURF = ("x1", "x0", "yl")
+ORDER = ("core", "z2", "yh", "z1", "z0", "x1", "x0", "yl")
+RUN, RUN_AXES = ("core", "z2", "yh", "z1", "z0"), ()
 NT_DIMS = (((1,), (1,)), ((), ()))
+
+
+def weight(axis):
+    return 1 << (len(ORDER) - 1 - ORDER.index(axis))
+
+
+def offset(axes, index):
+    return sum(weight(axis) * (index >> (len(axes) - 1 - i) & 1) for i, axis in enumerate(axes))
+
+
+def coordinate(axes):
+    index = 0
+    for axis in axes:
+        index = 2 * index + lax.axis_index(axis)
+    return index
 
 
 def fourier_tables(taps):
@@ -109,10 +128,19 @@
 
     for copy in copies[4:]:
         copy.wait()
-    place[...] = jnp.concatenate([plan[...] + i * plan.shape[1] for i in range(4)], axis=1)
+    slots = plan.shape[1]
+    lane = lax.broadcasted_iota(jnp.int32, (slots, LANES), 1)
+    source = jnp.zeros((slots, LANES), jnp.int32)
+    for i, axis in enumerate(RUN_AXES + RUN):
+        bit = (lane >> (len(SHOT) - 1 - i)) & 1
+        source = source + (bit << (len(SHOT) - 1 - SHOT.index(axis)))
+    chosen = (lax.broadcasted_iota(jnp.int32, (slots, LANES), 0) == source).astype(jnp.bfloat16)
+    panels = jnp.broadcast_to(plan[...].astype(jnp.bfloat16), (16, slots))
+    panel = jnp.dot(panels, chosen, preferred_element_type=jnp.float32)[:1].astype(jnp.int32)
+    place[...] = panel + lane[:1] // slots * slots
     for shot in range(shots):
         gain[pl.ds(shot, 1), :] = jnp.full((1, taps), scale[shot], jnp.float32)
-    first = lax.axis_index("surf") * position_count
+    first = coordinate(SURF) * position_count
     position = lax.broadcasted_iota(jnp.int32, (position_count, positions.shape[1]), 0) + first
     onehot = (position == positions[...]).astype(jnp.float32)
     halves_in_time = []
@@ -139,14 +167,20 @@
     rows[...] = received[...].astype(jnp.float32)
     chunk = received.shape[0] // (shot_devices * surf_devices)
     groups = width // 4
+    run, step = 1 << len(RUN), weight(RUN[-1])
+    starts = [offset(RUN_AXES, i) for i in range(1 << len(RUN_AXES))]
 
     def regrouped(row):
         halves = []
         for half in range(surf_devices // 4):
             parts = [
-                rows[pl.ds((half * 4 + i) * chunk + row, shot_devices, stride=surf_devices * chunk), :].astype(
-                    jnp.bfloat16
-                )
+                jnp.concatenate(
+                    [
+                        rows[pl.ds((start + offset(SURF, half * 4 + i)) * chunk + row, run, stride=step * chunk), :]
+                        for start in starts
+                    ],
+                    axis=0,
+                ).astype(jnp.bfloat16)
                 for i in range(4)
             ]
             halves.append(exchange_groups(parts))
@@ -159,8 +193,7 @@
             by_receiver += regrouped(part * groups + group)
         primary.append(by_receiver)
     traces = [jnp.concatenate(regrouped(2 * groups + part), axis=0) for part in range(2)]
-    frequency = lax.axis_index("shot") * surf_devices + lax.axis_index("surf")
-    interior = frequency > 0
+    interior = coordinate(ORDER) > 0
     pair = width // surf_devices
     for block in range(surf_devices):
         which = range(pair * block, pair * (block + 1))
@@ -175,9 +208,11 @@
             traces[0], with_real, NT_DIMS, preferred_element_type=jnp.float32
         ) + lax.dot_general(traces[1], with_imag, NT_DIMS, preferred_element_type=jnp.float32)
         for window in range(4):
-            packed[pl.ds(block * 4 + window, shot_devices, stride=surf_devices * 4), :] = product[
-                window * shot_devices : (window + 1) * shot_devices
-            ]
+            for i, start in enumerate(starts):
+                row = window * shot_devices + i * run
+                packed[pl.ds((start + offset(SURF, block)) * 4 + window, run, stride=step * 4), :] = product[
+                    row : row + run
+                ]
     sent[...] = packed[...].astype(jnp.bfloat16)
 
 
@@ -262,7 +297,7 @@
         )
     )
     sent = sent.reshape(devices, chunk // 2, 2, LANES)
-    received = lax.all_to_all(sent, ("shot", "surf"), 0, 0, tiled=True)
+    received = lax.all_to_all(sent, ORDER, 0, 0, tiled=True)
     received = received.reshape(devices * chunk, LANES)
 
     back = devices * 4
@@ -281,7 +316,7 @@
         ],
         compiler_params=limit,
     )(received)
-    terms = lax.all_to_all(terms.reshape(devices, 4, LANES), ("shot", "surf"), 0, 0, tiled=True)
+    terms = lax.all_to_all(terms.reshape(devices, 4, LANES), ORDER, 0, 0, tiled=True)
     terms = terms.reshape(back, LANES)
 
     return pl.pallas_call(
@@ -301,10 +336,12 @@
 def solution(mesh):
     P = jax.sharding.PartitionSpec
     shot_devices, surf_devices = mesh.shape["shot"], mesh.shape["surf"]
+    axes = SHOT + SURF
+    fine = jax.sharding.Mesh(mesh.devices.reshape((2,) * len(axes)), axes)
 
     def device(*args):
         return on_device(shot_devices, surf_devices, *args)
 
-    in_specs = (P("shot", "surf", None), P("surf"), P(), P("surf", None, "shot", None), P("shot"))
-    out_specs = P("shot", "surf", None)
-    return jax.shard_map(device, mesh=mesh, in_specs=in_specs, out_specs=out_specs, check_vma=False)
+    in_specs = (P(SHOT, SURF, None), P(SURF), P(), P(SURF, None, SHOT, None), P(SHOT))
+    out_specs = P(SHOT, SURF, None)
+    return jax.shard_map(device, mesh=fine, in_specs=in_specs, out_specs=out_specs, check_vma=False)

time: 64.9 us -> 64.1 us (0.988)
  blocking collectives: 60.2 us -> 59.3 us
    all_to_all x2, blocking collectives: 60.2 us -> 59.3 us  [the longest x1 38.2 us: on_device(): received = lax.all_to_all(sent, ORDER, 0, 0, tiled=True)]
where the time goes in v3:
time: 64.1 us; the launch traced here: 64 us
  blocking collectives  59.3 us (93%)
  Pallas kernels  4.59 us (7%)
    all_to_all x1, blocking collectives, on_device(): received = lax.all_to_all(sent, ORDER, 0, 0, tiled=True)  38.2 us
    all_to_all x1, blocking collectives, on_device(): lax.all_to_all(terms.reshape(devices, 4, LANES), ORDER, 0, 0, tiled=True)  21.1 us
    pallas_call x1, Pallas kernels, on_device(): pl.pallas_call(spectra_kernel, out_shape=(jax.ShapeDtypeStruct((taps * ch...  2.32 us

profile of v3, /device:TPU:1, one launch (start us, length us, event | category | flops | bytes accessed | tf_op | source)
XLA Modules:
  0.0 64.0 jit_solution(11947547024676459109)
XLA Ops:
  0.0 2.3 %shard_map.73 = (bf16[2560,128]{1,0:T(8,128)(2,1)S(1)}, s32[1,128]{1,0:T(1,128)S(1)}, f32[2,256]{1,0:T(2,128)S(1)}) custom-call(s32[1,64]{1,0:T(1,128)} %bitcast.12, s32[1,32]{1,0:T(1,128)} %bitcast.13, f32[2]{0:T(128)} %scale_in.1, f32[2,64,512]{2,1,0:T(8,128)} %data.1, bf16[32,16,256]{2,1,0:T(8,128)(2,1)} %bitcast.11, ...), custom_call_target="tpu_custom_call" | custom-call | tf_op jit(solution)/shard_map/pallas_call | solution.py:265
  2.3 38.2 %all_to_all.10 = bf16[256,5,2,128]{3,2,1,0:T(2,128)(2,1)S(1)} all-to-all(bf16[256,5,2,128]{3,2,1,0:T(2,128)(2,1)S(1)} %bitcast.10), channel_id=1, replica_groups=mesh['z2'=2,'z1'=2,'z0'=2,'yh'=2,'core'=2,'x1'=2,'x0'=2,'yl'=2] {'core',..., dimensions={0} | all-to-all | bytes 1310720 | tf_op jit(solution)/shard_map/all_to_all | solution.py:300
  40.5 1.1 %shard_map.74 = bf16[1024,128]{1,0:T(8,128)(2,1)S(1)} custom-call(bf16[2560,128]{1,0:T(8,128)(2,1)S(1)} %bitcast.7), custom_call_target="tpu_custom_call" | custom-call | tf_op jit(solution)/shard_map/pallas_call | solution.py:308
  41.7 0.0 copy-start
  41.7 0.0 copy-start.1
  41.7 21.1 %all_to_all.11 = bf16[256,4,128]{2,1,0:T(4,128)(2,1)S(1)} all-to-all(bf16[256,4,128]{2,1,0:T(4,128)(2,1)S(1)} %bitcast.8), channel_id=1, replica_groups=mesh['z2'=2,'z1'=2,'z0'=2,'yh'=2,'core'=2,'x1'=2,'x0'=2,'yl'=2] {'core',..., dimensions={0} | all-to-all | bytes 524288 | tf_op jit(solution)/shard_map/all_to_all | solution.py:319
  62.8 0.0 copy-done
  62.8 0.0 copy-done.1
  62.8 1.1 %shard_map.75 = f32[2,64,512]{2,1,0:T(8,128)} custom-call(s32[1,128]{1,0:T(1,128)S(1)} %get-tuple-element.8.place, f32[2,256]{1,0:T(2,128)S(1)} %get-tuple-element.9.gain, bf16[1024,128]{1,0:T(8,128)(2,1)S(1)} %bitcast.9, bf16[512,256]{1,0:T(8,128)(2,1)S(1)} %copy-done.1, f32[2,64,512]{2,1,0:T(8,128)S(1)} %copy-done), custom_call_target="tpu_custom_call" | custom-call | tf_op jit(solution)/shard_map/pallas_call | solution.py:322
Async XLA Ops:
  41.7 21.1 %copy-start = (f32[2,64,512]{2,1,0:T(8,128)S(1)}, f32[2,64,512]{2,1,0:T(8,128)}, u32[]{:S(2)}) copy-start(f32[2,64,512]{2,1,0:T(8,128)} %data.1) | copy-start | bytes 786436
  41.7 21.1 %copy-start.1 = (bf16[512,256]{1,0:T(8,128)(2,1)S(1)}, bf16[512,256]{1,0:T(8,128)(2,1)}, u32[]{:S(2)}) copy-start(bf16[512,256]{1,0:T(8,128)(2,1)} %constant.5.clone.inverse) | copy-start | bytes 786436

commit v4 on v3

--- a/solution.py
+++ b/solution.py
@@ -91,23 +91,38 @@
     chunk = packed.shape[0] // frequencies
     groups = width // 4
 
-    def halves(far, near):
-        half = far.shape[0] // 2
-        return [(far.at[pl.ds(i * half, half)], near.at[pl.ds(i * half, half)]) for i in range(2)]
-
-    pairs = halves(primaries_in, primaries) + halves(forward_in, forward) + halves(data_in, data)
-    pairs += [(positions_in, positions), (plan_in, plan), (scale_in, scale)]
+    pairs = [(data_in, data), (positions_in, positions), (primaries_in, primaries), (forward_in, forward)]
+    pairs += [(plan_in, plan), (scale_in, scale)]
     copies = [pltpu.make_async_copy(far, near, arrived.at[i]) for i, (far, near) in enumerate(pairs)]
     for copy in copies:
         copy.start()
 
-    for copy in copies[:2]:
+    for copy in copies[:1]:
+        copy.wait()
+    copies[1].wait()
+    first = coordinate(SURF) * position_count
+    receivers = positions.shape[1]
+    position = lax.broadcasted_iota(jnp.int32, (position_count, receivers), 0) + first
+    onehot = (position == positions[...]).astype(jnp.bfloat16)
+    onehot = jnp.concatenate([onehot] * 3, axis=1)
+    halves_in_time = []
+    for shot in range(shots):
+        parts, rest = [], data[shot]
+        for _ in range(3):
+            parts.append(rest.astype(jnp.bfloat16))
+            rest = rest - parts[-1].astype(jnp.float32)
+        gathered = jnp.dot(
+            onehot, jnp.concatenate(parts, axis=0), preferred_element_type=jnp.float32
+        ).astype(jnp.bfloat16)
+        halves_in_time += [gathered[:, :taps], gathered[:, taps:]]
+
+    for copy in copies[2:3]:
         copy.wait()
     flat = primaries[...].reshape(row_count, taps)
     tiles = range(taps // LANES)
     for tile in tiles:
         rows[tile] = flat[:, tile * LANES : (tile + 1) * LANES].astype(jnp.float32)
-    for copy in copies[2:4]:
+    for copy in copies[3:4]:
         copy.wait()
     for group in range(groups):
         block = jnp.concatenate(
@@ -140,15 +155,6 @@
     place[...] = panel + lane[:1] // slots * slots
     for shot in range(shots):
         gain[pl.ds(shot, 1), :] = jnp.full((1, taps), scale[shot], jnp.float32)
-    first = coordinate(SURF) * position_count
-    position = lax.broadcasted_iota(jnp.int32, (position_count, positions.shape[1]), 0) + first
-    onehot = (position == positions[...]).astype(jnp.float32)
-    halves_in_time = []
-    for shot in range(shots):
-        gathered = jnp.dot(
-            onehot, data[shot], precision=lax.Precision.HIGHEST, preferred_element_type=jnp.float32
-        ).astype(jnp.bfloat16)
-        halves_in_time += [gathered[:, :taps], gathered[:, taps:]]
     spectra = lax.dot_general(
         forward[...], jnp.concatenate(halves_in_time, axis=0), NT_DIMS, preferred_element_type=jnp.float32
     )
@@ -280,7 +286,7 @@
             pltpu.VMEM(forward.shape, jnp.bfloat16),
             pltpu.VMEM((taps // LANES, position_count * width, LANES), jnp.float32),
             pltpu.VMEM((taps * chunk, LANES), jnp.float32),
-            pltpu.SemaphoreType.DMA((9,)),
+            pltpu.SemaphoreType.DMA((6,)),
         ],
         compiler_params=limit,
     )(

time: 64.1 us -> 64 us (level)
  no operation moved by 1% of the time
where the time goes in v4:
time: 64 us; the launch traced here: 63.8 us
  blocking collectives  59.3 us (93%)
  Pallas kernels  4.46 us (7%)
    all_to_all x1, blocking collectives, on_device(): received = lax.all_to_all(sent, ORDER, 0, 0, tiled=True)  38.2 us
    all_to_all x1, blocking collectives, on_device(): lax.all_to_all(terms.reshape(devices, 4, LANES), ORDER, 0, 0, tiled=True)  21.1 us
    pallas_call x1, Pallas kernels, on_device(): pl.pallas_call(spectra_kernel, out_shape=(jax.ShapeDtypeStruct((taps * ch...  2.19 us

profile of v4, /device:TPU:1, one launch (start us, length us, event | category | flops | bytes accessed | tf_op | source)
XLA Modules:
  0.0 63.8 jit_solution(3626923060953682664)
XLA Ops:
  0.0 2.2 %shard_map.73 = (bf16[2560,128]{1,0:T(8,128)(2,1)S(1)}, s32[1,128]{1,0:T(1,128)S(1)}, f32[2,256]{1,0:T(2,128)S(1)}) custom-call(s32[1,64]{1,0:T(1,128)} %bitcast.12, s32[1,32]{1,0:T(1,128)} %bitcast.13, f32[2]{0:T(128)} %scale_in.1, f32[2,64,512]{2,1,0:T(8,128)} %data.1, bf16[32,16,256]{2,1,0:T(8,128)(2,1)} %bitcast.11, ...), custom_call_target="tpu_custom_call" | custom-call | tf_op jit(solution)/shard_map/pallas_call | solution.py:271
  2.2 38.2 %all_to_all.10 = bf16[256,5,2,128]{3,2,1,0:T(2,128)(2,1)S(1)} all-to-all(bf16[256,5,2,128]{3,2,1,0:T(2,128)(2,1)S(1)} %bitcast.10), channel_id=1, replica_groups=mesh['z2'=2,'z1'=2,'z0'=2,'yh'=2,'core'=2,'x1'=2,'x0'=2,'yl'=2] {'core',..., dimensions={0} | all-to-all | bytes 1310720 | tf_op jit(solution)/shard_map/all_to_all | solution.py:306
  40.4 1.1 %shard_map.74 = bf16[1024,128]{1,0:T(8,128)(2,1)S(1)} custom-call(bf16[2560,128]{1,0:T(8,128)(2,1)S(1)} %bitcast.7), custom_call_target="tpu_custom_call" | custom-call | tf_op jit(solution)/shard_map/pallas_call | solution.py:314
  41.6 0.0 copy-start
  41.6 0.0 copy-start.1
  41.6 21.1 %all_to_all.11 = bf16[256,4,128]{2,1,0:T(4,128)(2,1)S(1)} all-to-all(bf16[256,4,128]{2,1,0:T(4,128)(2,1)S(1)} %bitcast.8), channel_id=1, replica_groups=mesh['z2'=2,'z1'=2,'z0'=2,'yh'=2,'core'=2,'x1'=2,'x0'=2,'yl'=2] {'core',..., dimensions={0} | all-to-all | bytes 524288 | tf_op jit(solution)/shard_map/all_to_all | solution.py:325
  62.7 0.0 copy-done
  62.7 0.0 copy-done.1
  62.7 1.1 %shard_map.75 = f32[2,64,512]{2,1,0:T(8,128)} custom-call(s32[1,128]{1,0:T(1,128)S(1)} %get-tuple-element.8.place, f32[2,256]{1,0:T(2,128)S(1)} %get-tuple-element.9.gain, bf16[1024,128]{1,0:T(8,128)(2,1)S(1)} %bitcast.9, bf16[512,256]{1,0:T(8,128)(2,1)S(1)} %copy-done.1, f32[2,64,512]{2,1,0:T(8,128)S(1)} %copy-done), custom_call_target="tpu_custom_call" | custom-call | tf_op jit(solution)/shard_map/pallas_call | solution.py:328
Async XLA Ops:
  41.6 21.1 %copy-start = (f32[2,64,512]{2,1,0:T(8,128)S(1)}, f32[2,64,512]{2,1,0:T(8,128)}, u32[]{:S(2)}) copy-start(f32[2,64,512]{2,1,0:T(8,128)} %data.1) | copy-start | bytes 786436
  41.6 21.1 %copy-start.1 = (bf16[512,256]{1,0:T(8,128)(2,1)S(1)}, bf16[512,256]{1,0:T(8,128)(2,1)}, u32[]{:S(2)}) copy-start(bf16[512,256]{1,0:T(8,128)(2,1)} %constant.5.clone.inverse) | copy-start | bytes 786436

commit v5 on v4

--- a/solution.py
+++ b/solution.py
@@ -91,7 +91,9 @@
     chunk = packed.shape[0] // frequencies
     groups = width // 4
 
-    pairs = [(data_in, data), (positions_in, positions), (primaries_in, primaries), (forward_in, forward)]
+    spans = [pl.ds(part * frequencies, frequencies) for part in range(2)]
+    pairs = [(data_in, data), (positions_in, positions), (primaries_in, primaries)]
+    pairs += [(forward_in.at[span], forward.at[span]) for span in spans]
     pairs += [(plan_in, plan), (scale_in, scale)]
     copies = [pltpu.make_async_copy(far, near, arrived.at[i]) for i, (far, near) in enumerate(pairs)]
     for copy in copies:
@@ -122,8 +124,7 @@
     tiles = range(taps // LANES)
     for tile in tiles:
         rows[tile] = flat[:, tile * LANES : (tile + 1) * LANES].astype(jnp.float32)
-    for copy in copies[3:4]:
-        copy.wait()
+    blocks = []
     for group in range(groups):
         block = jnp.concatenate(
             [
@@ -135,13 +136,15 @@
             ],
             axis=0,
         ).astype(jnp.bfloat16)
-        spectra = lax.dot_general(forward[...], block, NT_DIMS, preferred_element_type=jnp.float32)
-        for part in range(2):
-            packed[pl.ds(part * groups + group, frequencies, stride=chunk), :] = spectra[
-                part * frequencies : (part + 1) * frequencies
-            ]
-
-    for copy in copies[4:]:
+        blocks.append(block)
+    for part, span in enumerate(spans):
+        copies[3 + part].wait()
+        for group, block in enumerate(blocks):
+            packed[pl.ds(part * groups + group, frequencies, stride=chunk), :] = lax.dot_general(
+                forward[span, :], block, NT_DIMS, preferred_element_type=jnp.float32
+            )
+
+    for copy in copies[5:]:
         copy.wait()
     slots = plan.shape[1]
     lane = lax.broadcasted_iota(jnp.int32, (slots, LANES), 1)
@@ -286,7 +289,7 @@
             pltpu.VMEM(forward.shape, jnp.bfloat16),
             pltpu.VMEM((taps // LANES, position_count * width, LANES), jnp.float32),
             pltpu.VMEM((taps * chunk, LANES), jnp.float32),
-            pltpu.SemaphoreType.DMA((6,)),
+            pltpu.SemaphoreType.DMA((7,)),
         ],
         compiler_params=limit,
     )(

time: 64 us -> 64.3 us (level)
  no operation moved by 1% of the time
where the time goes in v5:
time: 64.3 us; the launch traced here: 64.1 us
  blocking collectives  59.3 us (92%)
  Pallas kernels  4.75 us (7%)
    all_to_all x1, blocking collectives, on_device(): received = lax.all_to_all(sent, ORDER, 0, 0, tiled=True)  38.2 us
    all_to_all x1, blocking collectives, on_device(): lax.all_to_all(terms.reshape(devices, 4, LANES), ORDER, 0, 0, tiled=True)  21.1 us
    pallas_call x1, Pallas kernels, on_device(): pl.pallas_call(spectra_kernel, out_shape=(jax.ShapeDtypeStruct((taps * ch...  2.49 us

profile of v5, /device:TPU:1, one launch (start us, length us, event | category | flops | bytes accessed | tf_op | source)
XLA Modules:
  0.0 64.1 jit_solution(14771418086229547552)
XLA Ops:
  0.0 2.5 %shard_map.73 = (bf16[2560,128]{1,0:T(8,128)(2,1)S(1)}, s32[1,128]{1,0:T(1,128)S(1)}, f32[2,256]{1,0:T(2,128)S(1)}) custom-call(s32[1,64]{1,0:T(1,128)} %bitcast.12, s32[1,32]{1,0:T(1,128)} %bitcast.13, f32[2]{0:T(128)} %scale_in.1, f32[2,64,512]{2,1,0:T(8,128)} %data.1, bf16[32,16,256]{2,1,0:T(8,128)(2,1)} %bitcast.11, ...), custom_call_target="tpu_custom_call" | custom-call | tf_op jit(solution)/shard_map/pallas_call | solution.py:274
  2.5 38.2 %all_to_all.10 = bf16[256,5,2,128]{3,2,1,0:T(2,128)(2,1)S(1)} all-to-all(bf16[256,5,2,128]{3,2,1,0:T(2,128)(2,1)S(1)} %bitcast.10), channel_id=1, replica_groups=mesh['z2'=2,'z1'=2,'z0'=2,'yh'=2,'core'=2,'x1'=2,'x0'=2,'yl'=2] {'core',..., dimensions={0} | all-to-all | bytes 1310720 | tf_op jit(solution)/shard_map/all_to_all | solution.py:309
  40.7 1.1 %shard_map.74 = bf16[1024,128]{1,0:T(8,128)(2,1)S(1)} custom-call(bf16[2560,128]{1,0:T(8,128)(2,1)S(1)} %bitcast.7), custom_call_target="tpu_custom_call" | custom-call | tf_op jit(solution)/shard_map/pallas_call | solution.py:317
  41.9 0.0 copy-start
  41.9 0.0 copy-start.1
  41.9 21.1 %all_to_all.11 = bf16[256,4,128]{2,1,0:T(4,128)(2,1)S(1)} all-to-all(bf16[256,4,128]{2,1,0:T(4,128)(2,1)S(1)} %bitcast.8), channel_id=1, replica_groups=mesh['z2'=2,'z1'=2,'z0'=2,'yh'=2,'core'=2,'x1'=2,'x0'=2,'yl'=2] {'core',..., dimensions={0} | all-to-all | bytes 524288 | tf_op jit(solution)/shard_map/all_to_all | solution.py:328
  63.0 0.0 copy-done
  63.0 0.0 copy-done.1
  63.0 1.1 %shard_map.75 = f32[2,64,512]{2,1,0:T(8,128)} custom-call(s32[1,128]{1,0:T(1,128)S(1)} %get-tuple-element.8.place, f32[2,256]{1,0:T(2,128)S(1)} %get-tuple-element.9.gain, bf16[1024,128]{1,0:T(8,128)(2,1)S(1)} %bitcast.9, bf16[512,256]{1,0:T(8,128)(2,1)S(1)} %copy-done.1, f32[2,64,512]{2,1,0:T(8,128)S(1)} %copy-done), custom_call_target="tpu_custom_call" | custom-call | tf_op jit(solution)/shard_map/pallas_call | solution.py:331
Async XLA Ops:
  41.9 21.1 %copy-start = (f32[2,64,512]{2,1,0:T(8,128)S(1)}, f32[2,64,512]{2,1,0:T(8,128)}, u32[]{:S(2)}) copy-start(f32[2,64,512]{2,1,0:T(8,128)} %data.1) | copy-start | bytes 786436
  41.9 21.1 %copy-start.1 = (bf16[512,256]{1,0:T(8,128)(2,1)S(1)}, bf16[512,256]{1,0:T(8,128)(2,1)}, u32[]{:S(2)}) copy-start(bf16[512,256]{1,0:T(8,128)(2,1)} %constant.5.clone.inverse) | copy-start | bytes 786436
